TPU v7x, 32 devices: a whole 2x2x4 slice. The times are simulated.
32 devices in a mesh: grp: 2 (over y), ex: 4 (over z), layer: 4 (over x, core).
Axes of the slice: x: 2, y: 2, z: 4, core: 2. Of those that a mesh axis runs over, the one named last changes fastest.
Arguments:
- row_grads: bfloat16 [8, 16384, 1024], P('layer', ('grp', 'ex')), parts along dimension 1, may hold values from -0.1875 to 0.1875
- query_grads: bfloat16 [8, 256, 1024], P('layer', 'ex'), may hold values from -6 to 6
- fisher_inv: bfloat16 [8, 1024, 1024], P('layer'), as said below
Outputs:
- scores: float32 [16384, 256], P(('grp', 'ex'), 'layer'), parts along dimension 0
There are 2 independent parts, one for each index of `grp`. A program takes and returns all parts, laid end to end along the dimension named above; an argument that names none is the same for every part. Nothing has to cross between parts.
Inputs may be any that keep to these rules, and one draw needn't show every extreme that they name: `fisher_inv`: each layer's matrix is a positive multiple of one with diagonal entries near 2 and independent off-diagonal entries.
All inputs are finite; a program needn't handle non-finite values.
Results may differ from a plain program's by a relative error of at most 0.0029.
Values may be sent and summed in bfloat16 or wider, within the bound.
A program may use at most 128 MiB of HBM per device.

v0:
```python
import jax
import jax.numpy as jnp
from jax import lax
from jax.sharding import PartitionSpec as P


def precondition(queries, fisher_inv):
    return jnp.einsum(
        "lqk,ljk->lqj", queries, fisher_inv, preferred_element_type=jnp.float32
    ).astype(jnp.bfloat16)


def local(row_grads, query_grads, fisher_inv):
    prepared_own = precondition(query_grads, fisher_inv)
    partial_scores = jnp.einsum(
        "lrp,lqp->rq",
        row_grads,
        lax.all_gather(prepared_own, "ex", axis=1, tiled=True),
        preferred_element_type=jnp.float32,
    )
    return lax.psum_scatter(partial_scores, "layer", scatter_dimension=1, tiled=True)


def solution(mesh):
    in_specs = (P("layer", ("grp", "ex"), None), P("layer", "ex", None), P("layer", None, None))
    out_specs = P(("grp", "ex"), "layer")
    return jax.shard_map(local, mesh=mesh, in_specs=in_specs, out_specs=out_specs, check_vma=False)
```

profile of v0, /device:TPU:0, one launch (start us, length us, event | category | flops | bytes accessed | tf_op | source)
XLA Modules:
  0.0 87.9 jit_solution(2392732967696585509)
XLA Ops:
  6.5 0.0 copy-start
  6.5 0.0 all-gather.2.cloned.1.call-start
  6.5 0.9 %copy-done = bf16[2,64,1024]{2,1,0:T(8,128)(2,1)S(1)} copy-done((bf16[2,64,1024]{2,1,0:T(8,128)(2,1)S(1)}, bf16[2,64,1024]{2,1,0:T(8,128)(2,1)}, u32[]{:S(2)}) %copy-start) | copy-done | bytes 262168
  7.5 4.3 %convolution_convert_fusion = bf16[2,64,1024]{2,1,0:T(8,128)(2,1)} fusion(bf16[2,64,1024]{2,1,0:T(8,128)(2,1)S(1)} %copy-done, bf16[2,1024,1024]{2,1,0:T(8,128)(2,1)} %param.5), kind=kOutput, calls=%fused_computation.1 | convolution fusion | flops 268566528 | bytes 4718592 | tf_op jit(solution)/shard_map/lqk,ljk->lqj/dot_general | solution.py:8
  11.8 0.0 all-gather.2.cloned.1.call-update
  11.8 0.0 reduce-scatter.2.cloned.1.call-start
  11.8 30.7 %all-gather.2.cloned.1.call-done = bf16[2,256,1024]{2,1,0:T(8,128)(2,1)} async-done(((bf16[2,64,1024]{2,1,0:T(8,128)(2,1)}), bf16[2,256,1024]{2,1,0:T(8,128)(2,1)}) %all-gather.2.cloned.1.call-update) | async-done | bytes 1048592 | tf_op jit(solution)/shard_map/all_gather | solution.py:18
  42.6 7.4 %convolution_bitcast_fusion = f32[2048,256]{0,1:T(8,128)} fusion(bf16[2,256,1024]{2,1,0:T(8,128)(2,1)} %all-gather.2.cloned.1.call-done, bf16[2,2048,1024]{2,1,0:T(8,128)(2,1)} %param.3), kind=kOutput, calls=%fused_computation | convolution fusion | flops 2147483648 | bytes 11534336 | tf_op jit(solution)/shard_map/lrp,lqp->rq/dot_general | solution.py:15
  50.0 0.0 reduce-scatter.2.cloned.1.call-update
  50.0 31.1 %reduce-scatter.2.cloned.1.call-done = f32[2048,64]{0,1:T(8,128)} async-done(((f32[2048,256]{0,1:T(8,128)}), f32[2048,64]{0,1:T(8,128)}) %reduce-scatter.2.cloned.1.call-update) | async-done | bytes 524304 | tf_op jit(solution)/shard_map/reduce_scatter | solution.py:21
Async XLA Ops:
  6.5 1.0 %copy-start = (bf16[2,64,1024]{2,1,0:T(8,128)(2,1)S(1)}, bf16[2,64,1024]{2,1,0:T(8,128)(2,1)}, u32[]{:S(2)}) copy-start(bf16[2,64,1024]{2,1,0:T(8,128)(2,1)} %param.4) | copy-start | bytes 786436
  6.5 36.0 %all-gather.2.cloned.1.call-start = ((), (), s32[]{:S(2)}) async-start(), calls=%async_computation.1 | async-start | bytes 1310720 | tf_op jit(solution)/shard_map/all_gather | solution.py:18
  11.8 69.3 %reduce-scatter.2.cloned.1.call-start = ((), (), s32[]{:S(2)}) async-start(), calls=%async_computation.2 | async-start | bytes 2621440 | tf_op jit(solution)/shard_map/reduce_scatter | solution.py:21
Sparse Core Ops, SparseCore 0:
  11.9 30.6 all-gather.1
  50.1 30.9 reduce-scatter.1
where the time goes:
time: 88.1 us; the launch traced here: 87.9 us
  waiting for transfers between devices  61.8 us (70%)
  between operations  13.4 us (15%)
  matrix products  11.7 us (13%)
  local copies, waits for them, and re-layouts  0.95 us (1%)
    reduce_scatter x1, waiting for transfers between devices, local(): lax.psum_scatter(partial_scores, 'layer', scatter_dimension=1, tiled=True)  31.1 us
    all_gather x1, waiting for transfers between devices, local(): lax.all_gather(prepared_own, 'ex', axis=1, tiled=True)  30.7 us
    dot_general x1, matrix products, local(): jnp.einsum('lrp,lqp->rq', row_grads, lax.all_gather(prepared_own, 'ex', a...  7.41 us
    dot_general x1, matrix products, precondition(): jnp.einsum('lqk,ljk->lqj', queries, fisher_inv, preferred_element_type=jn...  4.28 us
  transfers between devices with their start and end apart: 2, of which 2 were waited for; matrix products, arithmetic and copies ran while one was open for 0% of the time, Pallas kernels for 0%

commit v1 on v0

v1 whole, which is shorter than its diff:
```python
import functools

import jax
import jax.numpy as jnp
from jax import lax
from jax.experimental import pallas as pl
from jax.experimental.pallas import tpu as pltpu
from jax.sharding import PartitionSpec as P

MESH = pl.DeviceIdType.MESH
CHUNKS = 4


def precondition(queries, fisher_inv):
    return jnp.einsum(
        "lqk,ljk->lqj", queries, fisher_inv, preferred_element_type=jnp.float32
    ).astype(jnp.bfloat16)


def plain(row_grads, query_grads, fisher_inv):
    prepared_own = precondition(query_grads, fisher_inv)
    partial_scores = jnp.einsum(
        "lrp,lqp->rq",
        row_grads,
        lax.all_gather(prepared_own, "ex", axis=1, tiled=True),
        preferred_element_type=jnp.float32,
    )
    return lax.psum_scatter(partial_scores, "layer", scatter_dimension=1, tiled=True)


def dot_nt(a, b):
    return lax.dot_general(a, b, (((1,), (1,)), ((), ())), preferred_element_type=jnp.float32)


def kernel(rows_hbm, q_hbm, f_hbm, out_ref,
           rows, q, fisher, prep, keep, send_a, recv_a, send_b, recv_b,
           load_sem, row_sem, z_send, z_recv, y_send, y_recv, a_send, a_recv, b_send, b_recv):
    y = lax.axis_index("grp")
    z = lax.axis_index("ex")
    i = lax.axis_index("layer")
    x = i // 2
    c = i - 2 * x
    other_core = 2 * x + 1 - c
    other_x = 2 * (1 - x) + c
    total = rows.shape[1]
    step = total // CHUNKS

    loads = [pltpu.make_async_copy(q_hbm, q, load_sem.at[2])]
    loads += [pltpu.make_async_copy(f_hbm.at[y], fisher.at[0], load_sem.at[0])]
    loads += [pltpu.make_async_copy(f_hbm.at[1 - y], fisher.at[1], load_sem.at[1])]
    for copy in loads:
        copy.start()

    def row_copy(n):
        part = pl.ds(n * step, step)
        return pltpu.make_async_copy(rows_hbm.at[:, part], rows.at[:, part], row_sem.at[n])

    for n in range(CHUNKS):
        row_copy(n).start()

    barrier = pltpu.get_barrier_semaphore()
    for d in (1, 2, 3):
        pl.semaphore_signal(barrier, inc=1, device_id={"ex": (z + d) % 4}, device_id_type=MESH)
    pl.semaphore_signal(barrier, inc=1, device_id={"grp": 1 - y}, device_id_type=MESH)
    pl.semaphore_signal(barrier, inc=1, device_id={"layer": other_core}, device_id_type=MESH)
    pl.semaphore_signal(barrier, inc=1, device_id={"layer": other_x}, device_id_type=MESH)

    side = z // 2
    w = z + side * (3 - 2 * z)
    order = [o + side * (3 - 2 * o) for o in (w, 1 - w, 2, 3)]

    def z_copy(k):
        return pltpu.make_async_remote_copy(
            src_ref=prep.at[z, y], dst_ref=prep.at[z, y],
            send_sem=z_send.at[order[k]], recv_sem=z_recv.at[z],
            device_id={"ex": order[k]}, device_id_type=MESH)

    def z_arrival(k):
        s = order[k]
        return pltpu.make_async_remote_copy(
            src_ref=prep.at[s, y], dst_ref=prep.at[s, y],
            send_sem=z_send.at[s], recv_sem=z_recv.at[s],
            device_id={"ex": s}, device_id_type=MESH)

    def y_copy(k, layer):
        s = order[k]
        return pltpu.make_async_remote_copy(
            src_ref=prep.at[s, layer], dst_ref=prep.at[s, layer],
            send_sem=y_send.at[s], recv_sem=y_recv.at[s],
            device_id={"grp": 1 - y}, device_id_type=MESH)

    loads[0].wait()
    loads[1].wait()
    prep[z, y] = dot_nt(q[y], fisher[0]).astype(jnp.bfloat16)
    pl.semaphore_wait(barrier, 6)
    for k in (1, 2, 3):
        z_copy(k).start()
    loads[2].wait()
    prep[z, 1 - y] = dot_nt(q[1 - y], fisher[1]).astype(jnp.bfloat16)

    def a_copy(xi, n):
        part = pl.ds(pl.multiple_of(n * step, step), step)
        return pltpu.make_async_remote_copy(
            src_ref=send_a.at[xi, :, part], dst_ref=recv_a.at[xi, :, part],
            send_sem=a_send.at[xi, n], recv_sem=a_recv.at[xi, n],
            device_id={"layer": other_core}, device_id_type=MESH)

    def b_copy(n):
        part = pl.ds(pl.multiple_of(n * step, step), step)
        return pltpu.make_async_remote_copy(
            src_ref=send_b.at[:, part], dst_ref=recv_b.at[:, part],
            send_sem=b_send.at[n], recv_sem=b_recv.at[n],
            device_id={"layer": other_x}, device_id_type=MESH)

    def compute(k):
        s = order[k]
        xi = s // 2
        ci = s - 2 * xi

        @pl.loop(0, CHUNKS)
        def _(n):
            if k == 0:
                row_copy(n).wait()
            part = pl.ds(pl.multiple_of(n * step, step), step)
            value = dot_nt(prep[s, 0], rows[0, part]) + dot_nt(prep[s, 1], rows[1, part])

            @pl.when(ci == c)
            def _():
                keep[xi, :, part] = value

            @pl.when(ci != c)
            def _():
                send_a[xi, :, part] = value.astype(jnp.bfloat16)
                a_copy(xi, n).start()

    def reduce(k):
        s = order[k]
        xi = s // 2
        ci = s - 2 * xi

        @pl.when(ci == c)
        def _():
            @pl.loop(0, CHUNKS)
            def _(n):
                part = pl.ds(pl.multiple_of(n * step, step), step)
                a_copy(xi, n).wait_recv()
                value = keep[xi, :, part] + recv_a[xi, :, part].astype(jnp.float32)

                @pl.when(xi == x)
                def _():
                    out_ref[:, part] = value

                @pl.when(xi != x)
                def _():
                    send_b[:, part] = value.astype(jnp.bfloat16)
                    b_copy(n).start()

    def pass_on(k):
        z_arrival(k).wait_recv()
        y_copy(k, y).start()

    compute(0)
    pass_on(1)
    reduce(0)
    pass_on(2)
    y_copy(1, 1 - y).wait_recv()
    compute(1)
    pass_on(3)
    reduce(1)
    y_copy(2, 1 - y).wait_recv()
    compute(2)
    reduce(2)
    y_copy(3, 1 - y).wait_recv()
    compute(3)
    reduce(3)

    @pl.loop(0, CHUNKS)
    def _(n):
        part = pl.ds(pl.multiple_of(n * step, step), step)
        b_copy(n).wait_recv()
        out_ref[:, part] += recv_b[:, part].astype(jnp.float32)

    for k in (1, 2, 3):
        z_copy(k).wait_send()
        y_copy(k, y).wait_send()

    @pl.loop(0, CHUNKS)
    def _(n):
        a_copy(0, n).wait_send()
        a_copy(1, n).wait_send()
        b_copy(n).wait_send()


def fused(row_grads, query_grads, fisher_inv):
    layers, total, depth = row_grads.shape
    queries = query_grads.shape[1]
    bf16 = jnp.bfloat16
    dma = pltpu.SemaphoreType.DMA
    out = pl.pallas_call(
        kernel,
        out_shape=jax.ShapeDtypeStruct((queries, total), jnp.float32),
        in_specs=[pl.BlockSpec(memory_space=pl.ANY)] * 3,
        out_specs=pl.BlockSpec(memory_space=pltpu.VMEM),
        scratch_shapes=[
            pltpu.VMEM((layers, total, depth), bf16),
            pltpu.VMEM((layers, queries, depth), bf16),
            pltpu.VMEM((layers, depth, depth), bf16),
            pltpu.VMEM((4, layers, queries, depth), bf16),
            pltpu.VMEM((2, queries, total), jnp.float32),
            pltpu.VMEM((2, queries, total), bf16),
            pltpu.VMEM((2, queries, total), bf16),
            pltpu.VMEM((queries, total), bf16),
            pltpu.VMEM((queries, total), bf16),
            dma((3,)), dma((CHUNKS,)),
            dma((4,)), dma((4,)), dma((4,)), dma((4,)),
            dma((2, CHUNKS)), dma((2, CHUNKS)), dma((CHUNKS,)), dma((CHUNKS,)),
        ],
        compiler_params=pltpu.CompilerParams(
            collective_id=0, has_side_effects=True, vmem_limit_bytes=40 * 2**20
        ),
    )(row_grads, query_grads, fisher_inv)
    return out.T


def solution(mesh):
    in_specs = (P("layer", ("grp", "ex"), None), P("layer", "ex", None), P("layer", None, None))
    out_specs = P(("grp", "ex"), "layer")

    def run(row_grads, query_grads, fisher_inv):
        two_layers = row_grads.shape[0] == 8
        small = (mesh.shape["grp"], mesh.shape["ex"], mesh.shape["layer"]) == (2, 4, 4)
        local = fused if small and two_layers else plain
        return jax.shard_map(
            local, mesh=mesh, in_specs=in_specs, out_specs=out_specs, check_vma=False
        )(row_grads, query_grads, fisher_inv)

    return run
```

time: 88.1 us -> 40 us (0.45)
  the two profiles are of different devices: /device:TPU:0 before, /device:TPU:24 now
where the time goes in v1:
time: 40 us; the launch traced here: 39.7 us
  Pallas kernels  32.3 us (81%)
  local copies, waits for them, and re-layouts  7.31 us (18%)
    pallas_call x1, Pallas kernels, fused(): pl.pallas_call(kernel, out_shape=jax.ShapeDtypeStruct((queries, total), j...  32.3 us
    unnamed x7, local copies, waits for them, and re-layouts  7.31 us

profile of v1, /device:TPU:24, one launch (start us, length us, event | category | flops | bytes accessed | tf_op | source)
XLA Modules:
  0.0 39.7 jit_solution(18251257616282486743)
XLA Ops:
  0.0 0.0 copy-start
  0.0 3.4 %copy-done = bf16[2,2048,1024]{2,1,0:T(8,128)(2,1)S(1)} copy-done((bf16[2,2048,1024]{2,1,0:T(8,128)(2,1)S(1)}, bf16[2,2048,1024]{2,1,0:T(8,128)(2,1)}, u32[]{:S(2)}) %copy-start) | copy-done | bytes 8388632
  3.4 0.0 copy-start.1
  3.4 2.2 %copy-done.1 = bf16[2,1024,1024]{2,1,0:T(8,128)(2,1)S(1)} copy-done((bf16[2,1024,1024]{2,1,0:T(8,128)(2,1)S(1)}, bf16[2,1024,1024]{2,1,0:T(8,128)(2,1)}, u32[]{:S(2)}) %copy-start.1) | copy-done | bytes 4194328
  5.6 0.0 copy-start.2
  5.6 0.9 %copy-done.2 = bf16[2,64,1024]{2,1,0:T(8,128)(2,1)S(1)} copy-done((bf16[2,64,1024]{2,1,0:T(8,128)(2,1)S(1)}, bf16[2,64,1024]{2,1,0:T(8,128)(2,1)}, u32[]{:S(2)}) %copy-start.2) | copy-done | bytes 262168
  6.5 32.3 %shard_map.37 = f32[64,2048]{1,0:T(8,128)S(1)} custom-call(bf16[2,2048,1024]{2,1,0:T(8,128)(2,1)S(1)} %copy-done, bf16[2,64,1024]{2,1,0:T(8,128)(2,1)S(1)} %copy-done.2, bf16[2,1024,1024]{2,1,0:T(8,128)(2,1)S(1)} %copy-done.1), custom_call_target="tpu_custom_call" | custom-call | tf_op jit(solution)/shard_map/pallas_call | solution.py:199
  38.9 0.8 %copy.5 = f32[2048,64]{0,1:T(8,128)} copy(f32[2048,64]{0,1:T(8,128)S(1)} %bitcast.1) | data formatting | bytes 1048576
Async XLA Ops:
  0.0 3.4 %copy-start = (bf16[2,2048,1024]{2,1,0:T(8,128)(2,1)S(1)}, bf16[2,2048,1024]{2,1,0:T(8,128)(2,1)}, u32[]{:S(2)}) copy-start(bf16[2,2048,1024]{2,1,0:T(8,128)(2,1)} %rows_hbm.1) | copy-start | bytes 25165828
  3.4 2.2 %copy-start.1 = (bf16[2,1024,1024]{2,1,0:T(8,128)(2,1)S(1)}, bf16[2,1024,1024]{2,1,0:T(8,128)(2,1)}, u32[]{:S(2)}) copy-start(bf16[2,1024,1024]{2,1,0:T(8,128)(2,1)} %f_hbm.1) | copy-start | bytes 12582916
  5.6 0.9 %copy-start.2 = (bf16[2,64,1024]{2,1,0:T(8,128)(2,1)S(1)}, bf16[2,64,1024]{2,1,0:T(8,128)(2,1)}, u32[]{:S(2)}) copy-start(bf16[2,64,1024]{2,1,0:T(8,128)(2,1)} %q_hbm.1) | copy-start | bytes 786436

commit v2 on v1

--- a/solution.py
+++ b/solution.py
@@ -9,6 +9,7 @@
 
 MESH = pl.DeviceIdType.MESH
 CHUNKS = 4
+HALVES = 2
 
 
 def precondition(queries, fisher_inv):
@@ -33,7 +34,7 @@
 
 
 def kernel(rows_hbm, q_hbm, f_hbm, out_ref,
-           rows, q, fisher, prep, keep, send_a, recv_a, send_b, recv_b,
+           rows, q, fisher, prep, acc, keep, send_a, recv_a, send_b, recv_b,
            load_sem, row_sem, z_send, z_recv, y_send, y_recv, a_send, a_recv, b_send, b_recv):
     y = lax.axis_index("grp")
     z = lax.axis_index("ex")
@@ -44,6 +45,12 @@
     other_x = 2 * (1 - x) + c
     total = rows.shape[1]
     step = total // CHUNKS
+    half = q.shape[1] // HALVES
+
+    side = z // 2
+    w = z + side * (3 - 2 * z)
+    mid = w == 1
+    order = [o + side * (3 - 2 * o) for o in (w, 1 - w, 2, 3)]
 
     loads = [pltpu.make_async_copy(q_hbm, q, load_sem.at[2])]
     loads += [pltpu.make_async_copy(f_hbm.at[y], fisher.at[0], load_sem.at[0])]
@@ -55,46 +62,61 @@
         part = pl.ds(n * step, step)
         return pltpu.make_async_copy(rows_hbm.at[:, part], rows.at[:, part], row_sem.at[n])
 
+    barrier = pltpu.get_barrier_semaphore()
+
+    def greet(**device):
+        pl.semaphore_signal(barrier, inc=1, device_id=device, device_id_type=MESH)
+
+    greet(ex=order[1])
+
+    @pl.when(mid)
+    def _():
+        greet(ex=order[2])
+
+    greet(grp=1 - y)
+    greet(layer=other_core)
+    greet(layer=other_x)
+
+    def z_copy(shard, to, slot, h):
+        part = pl.ds(h * half, half)
+        return pltpu.make_async_remote_copy(
+            src_ref=prep.at[shard, y, part], dst_ref=prep.at[shard, y, part],
+            send_sem=z_send.at[slot, h], recv_sem=z_recv.at[shard, h],
+            device_id={"ex": to}, device_id_type=MESH)
+
+    def y_copy(k, layer, h):
+        s = order[k]
+        part = pl.ds(h * half, half)
+        return pltpu.make_async_remote_copy(
+            src_ref=prep.at[s, layer, part], dst_ref=prep.at[s, layer, part],
+            send_sem=y_send.at[k, h], recv_sem=y_recv.at[k, h],
+            device_id={"grp": 1 - y}, device_id_type=MESH)
+
+    onward = {1: order[2], 2: order[1], 3: order[1]}
+
+    def pass_on(k):
+        for h in range(HALVES):
+            z_copy(order[k], order[1], 1 + k, h).wait_recv()
+
+            @pl.when(mid)
+            def _():
+                z_copy(order[k], onward[k], 1 + k, h).start()
+
+            y_copy(k, y, h).start()
+
+    loads[0].wait()
+    loads[1].wait()
     for n in range(CHUNKS):
         row_copy(n).start()
-
-    barrier = pltpu.get_barrier_semaphore()
-    for d in (1, 2, 3):
-        pl.semaphore_signal(barrier, inc=1, device_id={"ex": (z + d) % 4}, device_id_type=MESH)
-    pl.semaphore_signal(barrier, inc=1, device_id={"grp": 1 - y}, device_id_type=MESH)
-    pl.semaphore_signal(barrier, inc=1, device_id={"layer": other_core}, device_id_type=MESH)
-    pl.semaphore_signal(barrier, inc=1, device_id={"layer": other_x}, device_id_type=MESH)
-
-    side = z // 2
-    w = z + side * (3 - 2 * z)
-    order = [o + side * (3 - 2 * o) for o in (w, 1 - w, 2, 3)]
-
-    def z_copy(k):
-        return pltpu.make_async_remote_copy(
-            src_ref=prep.at[z, y], dst_ref=prep.at[z, y],
-            send_sem=z_send.at[order[k]], recv_sem=z_recv.at[z],
-            device_id={"ex": order[k]}, device_id_type=MESH)
-
-    def z_arrival(k):
-        s = order[k]
-        return pltpu.make_async_remote_copy(
-            src_ref=prep.at[s, y], dst_ref=prep.at[s, y],
-            send_sem=z_send.at[s], recv_sem=z_recv.at[s],
-            device_id={"ex": s}, device_id_type=MESH)
-
-    def y_copy(k, layer):
-        s = order[k]
-        return pltpu.make_async_remote_copy(
-            src_ref=prep.at[s, layer], dst_ref=prep.at[s, layer],
-            send_sem=y_send.at[s], recv_sem=y_recv.at[s],
-            device_id={"grp": 1 - y}, device_id_type=MESH)
-
-    loads[0].wait()
-    loads[1].wait()
     prep[z, y] = dot_nt(q[y], fisher[0]).astype(jnp.bfloat16)
-    pl.semaphore_wait(barrier, 6)
-    for k in (1, 2, 3):
-        z_copy(k).start()
+    pl.semaphore_wait(barrier, 4 + w)
+    for h in range(HALVES):
+        z_copy(z, order[1], 0, h).start()
+
+        @pl.when(mid)
+        def _():
+            z_copy(z, order[2], 1, h).start()
+
     loads[2].wait()
     prep[z, 1 - y] = dot_nt(q[1 - y], fisher[1]).astype(jnp.bfloat16)
 
@@ -112,17 +134,25 @@
             send_sem=b_send.at[n], recv_sem=b_recv.at[n],
             device_id={"layer": other_x}, device_id_type=MESH)
 
-    def compute(k):
+    def first(k):
+        @pl.loop(0, CHUNKS)
+        def _(n):
+            part = pl.ds(pl.multiple_of(n * step, step), step)
+            acc[k - 1, :, part] = dot_nt(prep[order[k], y], rows[y, part])
+
+    def second(k):
         s = order[k]
         xi = s // 2
         ci = s - 2 * xi
 
         @pl.loop(0, CHUNKS)
         def _(n):
+            part = pl.ds(pl.multiple_of(n * step, step), step)
             if k == 0:
                 row_copy(n).wait()
-            part = pl.ds(pl.multiple_of(n * step, step), step)
-            value = dot_nt(prep[s, 0], rows[0, part]) + dot_nt(prep[s, 1], rows[1, part])
+                value = dot_nt(prep[s, 0], rows[0, part]) + dot_nt(prep[s, 1], rows[1, part])
+            else:
+                value = acc[k - 1, :, part] + dot_nt(prep[s, 1 - y], rows[1 - y, part])
 
             @pl.when(ci == c)
             def _():
@@ -132,6 +162,10 @@
             def _():
                 send_a[xi, :, part] = value.astype(jnp.bfloat16)
                 a_copy(xi, n).start()
+
+    def swapped(k):
+        for h in range(HALVES):
+            y_copy(k, 1 - y, h).wait_recv()
 
     def reduce(k):
         s = order[k]
@@ -155,23 +189,39 @@
                     send_b[:, part] = value.astype(jnp.bfloat16)
                     b_copy(n).start()
 
-    def pass_on(k):
-        z_arrival(k).wait_recv()
-        y_copy(k, y).start()
-
-    compute(0)
+    second(0)
     pass_on(1)
+
+    @pl.when(mid)
+    def _():
+        pass_on(2)
+
     reduce(0)
-    pass_on(2)
-    y_copy(1, 1 - y).wait_recv()
-    compute(1)
-    pass_on(3)
+    first(1)
+
+    @pl.when(mid)
+    def _():
+        pass_on(3)
+
+    @pl.when(jnp.logical_not(mid))
+    def _():
+        pass_on(2)
+
+    first(2)
+    swapped(1)
+    second(1)
+
+    @pl.when(jnp.logical_not(mid))
+    def _():
+        pass_on(3)
+
+    first(3)
     reduce(1)
-    y_copy(2, 1 - y).wait_recv()
-    compute(2)
+    swapped(2)
+    second(2)
     reduce(2)
-    y_copy(3, 1 - y).wait_recv()
-    compute(3)
+    swapped(3)
+    second(3)
     reduce(3)
 
     @pl.loop(0, CHUNKS)
@@ -180,9 +230,16 @@
         b_copy(n).wait_recv()
         out_ref[:, part] += recv_b[:, part].astype(jnp.float32)
 
-    for k in (1, 2, 3):
-        z_copy(k).wait_send()
-        y_copy(k, y).wait_send()
+    for h in range(HALVES):
+        z_copy(z, order[1], 0, h).wait_send()
+        for k in (1, 2, 3):
+            y_copy(k, y, h).wait_send()
+
+        @pl.when(mid)
+        def _():
+            z_copy(z, order[2], 1, h).wait_send()
+            for k in (1, 2, 3):
+                z_copy(order[k], onward[k], 1 + k, h).wait_send()
 
     @pl.loop(0, CHUNKS)
     def _(n):
@@ -206,17 +263,18 @@
             pltpu.VMEM((layers, queries, depth), bf16),
             pltpu.VMEM((layers, depth, depth), bf16),
             pltpu.VMEM((4, layers, queries, depth), bf16),
+            pltpu.VMEM((3, queries, total), jnp.float32),
             pltpu.VMEM((2, queries, total), jnp.float32),
             pltpu.VMEM((2, queries, total), bf16),
             pltpu.VMEM((2, queries, total), bf16),
             pltpu.VMEM((queries, total), bf16),
             pltpu.VMEM((queries, total), bf16),
             dma((3,)), dma((CHUNKS,)),
-            dma((4,)), dma((4,)), dma((4,)), dma((4,)),
+            dma((5, HALVES)), dma((4, HALVES)), dma((4, HALVES)), dma((4, HALVES)),
             dma((2, CHUNKS)), dma((2, CHUNKS)), dma((CHUNKS,)), dma((CHUNKS,)),
         ],
         compiler_params=pltpu.CompilerParams(
-            collective_id=0, has_side_effects=True, vmem_limit_bytes=40 * 2**20
+            collective_id=0, has_side_effects=True, vmem_limit_bytes=60 * 2**20
         ),
     )(row_grads, query_grads, fisher_inv)
     return out.T

time: 40 us -> 31.2 us (0.78)
  local copies, waits for them, and re-layouts: 7.31 us -> 1.87 us
  Pallas kernels: 32.3 us -> 29.1 us
    unnamed x7 -> x1, local copies, waits for them, and re-layouts: 7.31 us -> 1.87 us
    pallas_call x1, Pallas kernels: 32.3 us -> 29.1 us  [fused(): pl.pallas_call(kernel, out_shape=jax.ShapeDtypeStruct((queries, total), j...]
where the time goes in v2:
time: 31.2 us; the launch traced here: 31 us
  Pallas kernels  29.1 us (93%)
  local copies, waits for them, and re-layouts  1.87 us (6%)
    pallas_call x1, Pallas kernels, fused(): pl.pallas_call(kernel, out_shape=jax.ShapeDtypeStruct((queries, total), j...  29.1 us
    unnamed x1, local copies, waits for them, and re-layouts  1.87 us

profile of v2, /device:TPU:24, one launch (start us, length us, event | category | flops | bytes accessed | tf_op | source)
XLA Modules:
  0.0 31.0 jit_solution(10419209173269584873)
XLA Ops:
  0.0 29.1 %shard_map.37 = f32[64,2048]{1,0:T(8,128)} custom-call(bf16[2,2048,1024]{2,1,0:T(8,128)(2,1)} %rows_hbm.1, bf16[2,64,1024]{2,1,0:T(8,128)(2,1)} %q_hbm.1, bf16[2,1024,1024]{2,1,0:T(8,128)(2,1)} %f_hbm.1), custom_call_target="tpu_custom_call" | custom-call | tf_op jit(solution)/shard_map/pallas_call | solution.py:256
  29.2 1.9 %copy.5 = f32[2048,64]{0,1:T(8,128)} copy(f32[2048,64]{0,1:T(8,128)} %bitcast.1) | data formatting | bytes 1048576

commit v3 on v2

--- a/solution.py
+++ b/solution.py
@@ -8,7 +8,8 @@
 from jax.sharding import PartitionSpec as P
 
 MESH = pl.DeviceIdType.MESH
-CHUNKS = 4
+CHUNKS = 2
+LAST_CHUNKS = 2
 HALVES = 2
 
 
@@ -120,83 +121,92 @@
     loads[2].wait()
     prep[z, 1 - y] = dot_nt(q[1 - y], fisher[1]).astype(jnp.bfloat16)
 
-    def a_copy(xi, n):
-        part = pl.ds(pl.multiple_of(n * step, step), step)
+    def tile(k, h, r):
+        if k < 3:
+            queries, chunks = pl.ds(0, half * HALVES), CHUNKS
+        else:
+            queries, chunks = pl.ds(h * half, half), LAST_CHUNKS
+        size = total // chunks
+        return queries, pl.ds(pl.multiple_of(r * size, size), size), h * chunks + r
+
+    def place(k):
+        s = order[k]
+        return s, s // 2, s - 2 * (s // 2)
+
+    def a_copy(k, h, r):
+        xi = place(k)[1]
+        queries, part, n = tile(k, h, r)
         return pltpu.make_async_remote_copy(
-            src_ref=send_a.at[xi, :, part], dst_ref=recv_a.at[xi, :, part],
+            src_ref=send_a.at[xi, queries, part], dst_ref=recv_a.at[xi, queries, part],
             send_sem=a_send.at[xi, n], recv_sem=a_recv.at[xi, n],
             device_id={"layer": other_core}, device_id_type=MESH)
 
-    def b_copy(n):
-        part = pl.ds(pl.multiple_of(n * step, step), step)
+    def b_copy(k, h, r):
+        queries, part, n = tile(k, h, r)
         return pltpu.make_async_remote_copy(
-            src_ref=send_b.at[:, part], dst_ref=recv_b.at[:, part],
+            src_ref=send_b.at[queries, part], dst_ref=recv_b.at[queries, part],
             send_sem=b_send.at[n], recv_sem=b_recv.at[n],
             device_id={"layer": other_x}, device_id_type=MESH)
 
     def first(k):
         @pl.loop(0, CHUNKS)
-        def _(n):
-            part = pl.ds(pl.multiple_of(n * step, step), step)
+        def _(r):
+            part = pl.ds(pl.multiple_of(r * step, step), step)
             acc[k - 1, :, part] = dot_nt(prep[order[k], y], rows[y, part])
 
-    def second(k):
-        s = order[k]
-        xi = s // 2
-        ci = s - 2 * xi
-
-        @pl.loop(0, CHUNKS)
-        def _(n):
-            part = pl.ds(pl.multiple_of(n * step, step), step)
-            if k == 0:
-                row_copy(n).wait()
-                value = dot_nt(prep[s, 0], rows[0, part]) + dot_nt(prep[s, 1], rows[1, part])
-            else:
-                value = acc[k - 1, :, part] + dot_nt(prep[s, 1 - y], rows[1 - y, part])
-
-            @pl.when(ci == c)
+    def second(k, h, r):
+        s, xi, ci = place(k)
+        queries, part, _ = tile(k, h, r)
+        if k == 0:
+            row_copy(r).wait()
+            value = dot_nt(prep[s, 0], rows[0, part]) + dot_nt(prep[s, 1], rows[1, part])
+        else:
+            value = acc[k - 1, queries, part] + dot_nt(prep[s, 1 - y, queries], rows[1 - y, part])
+
+        @pl.when(ci == c)
+        def _():
+            keep[xi, queries, part] = value
+
+        @pl.when(ci != c)
+        def _():
+            send_a[xi, queries, part] = value.astype(jnp.bfloat16)
+            a_copy(k, h, r).start()
+
+    def reduce(k, h, r):
+        s, xi, ci = place(k)
+        queries, part, _ = tile(k, h, r)
+
+        @pl.when(ci == c)
+        def _():
+            a_copy(k, h, r).wait_recv()
+            value = keep[xi, queries, part] + recv_a[xi, queries, part].astype(jnp.float32)
+
+            @pl.when(xi == x)
             def _():
-                keep[xi, :, part] = value
-
-            @pl.when(ci != c)
+                out_ref[queries, part] = value
+
+            @pl.when(xi != x)
             def _():
-                send_a[xi, :, part] = value.astype(jnp.bfloat16)
-                a_copy(xi, n).start()
-
-    def swapped(k):
-        for h in range(HALVES):
-            y_copy(k, 1 - y, h).wait_recv()
-
-    def reduce(k):
-        s = order[k]
-        xi = s // 2
-        ci = s - 2 * xi
-
-        @pl.when(ci == c)
-        def _():
-            @pl.loop(0, CHUNKS)
-            def _(n):
-                part = pl.ds(pl.multiple_of(n * step, step), step)
-                a_copy(xi, n).wait_recv()
-                value = keep[xi, :, part] + recv_a[xi, :, part].astype(jnp.float32)
-
-                @pl.when(xi == x)
-                def _():
-                    out_ref[:, part] = value
-
-                @pl.when(xi != x)
-                def _():
-                    send_b[:, part] = value.astype(jnp.bfloat16)
-                    b_copy(n).start()
-
-    second(0)
+                send_b[queries, part] = value.astype(jnp.bfloat16)
+                b_copy(k, h, r).start()
+
+    def each(k, *steps):
+        @pl.loop(0, CHUNKS if k < 3 else LAST_CHUNKS)
+        def _(r):
+            for work, h in steps:
+                work(k, h, r)
+
+    def swapped(k, h):
+        y_copy(k, 1 - y, h).wait_recv()
+
+    each(0, (second, 0))
     pass_on(1)
 
     @pl.when(mid)
     def _():
         pass_on(2)
 
-    reduce(0)
+    each(0, (reduce, 0))
     first(1)
 
     @pl.when(mid)
@@ -208,27 +218,54 @@
         pass_on(2)
 
     first(2)
-    swapped(1)
-    second(1)
+    for h in range(HALVES):
+        swapped(1, h)
+    each(1, (second, 0))
 
     @pl.when(jnp.logical_not(mid))
     def _():
         pass_on(3)
 
     first(3)
-    reduce(1)
-    swapped(2)
-    second(2)
-    reduce(2)
-    swapped(3)
-    second(3)
-    reduce(3)
-
-    @pl.loop(0, CHUNKS)
-    def _(n):
-        part = pl.ds(pl.multiple_of(n * step, step), step)
-        b_copy(n).wait_recv()
-        out_ref[:, part] += recv_b[:, part].astype(jnp.float32)
+    each(1, (reduce, 0))
+    for h in range(HALVES):
+        swapped(2, h)
+    each(2, (second, 0))
+    each(2, (reduce, 0))
+    for h in range(HALVES):
+        swapped(3, h)
+        each(3, (second, h), *([(reduce, h - 1)] if h else []))
+    each(3, (reduce, HALVES - 1))
+
+    def finish(k, h, r):
+        queries, part, _ = tile(k, h, r)
+        b_copy(k, h, r).wait_recv()
+        out_ref[queries, part] += recv_b[queries, part].astype(jnp.float32)
+
+    def a_sent(k, h, r):
+        a_copy(k, h, r).wait_send()
+
+    def b_sent(k, h, r):
+        b_copy(k, h, r).wait_send()
+
+    for k in range(4):
+        s, xi, ci = place(k)
+        parts = range(HALVES if k == 3 else 1)
+
+        @pl.when(s == i)
+        def _():
+            for h in parts:
+                each(k, (finish, h))
+
+        @pl.when(ci != c)
+        def _():
+            for h in parts:
+                each(k, (a_sent, h))
+
+        @pl.when(s == other_x)
+        def _():
+            for h in parts:
+                each(k, (b_sent, h))
 
     for h in range(HALVES):
         z_copy(z, order[1], 0, h).wait_send()
@@ -240,12 +277,6 @@
             z_copy(z, order[2], 1, h).wait_send()
             for k in (1, 2, 3):
                 z_copy(order[k], onward[k], 1 + k, h).wait_send()
-
-    @pl.loop(0, CHUNKS)
-    def _(n):
-        a_copy(0, n).wait_send()
-        a_copy(1, n).wait_send()
-        b_copy(n).wait_send()
 
 
 def fused(row_grads, query_grads, fisher_inv):
@@ -253,10 +284,11 @@
     queries = query_grads.shape[1]
     bf16 = jnp.bfloat16
     dma = pltpu.SemaphoreType.DMA
+    tiles = max(CHUNKS, HALVES * LAST_CHUNKS)
     out = pl.pallas_call(
         kernel,
         out_shape=jax.ShapeDtypeStruct((queries, total), jnp.float32),
-        in_specs=[pl.BlockSpec(memory_space=pl.ANY)] * 3,
+        in_specs=[pl.BlockSpec(memory_space=pltpu.HBM)] * 3,
         out_specs=pl.BlockSpec(memory_space=pltpu.VMEM),
         scratch_shapes=[
             pltpu.VMEM((layers, total, depth), bf16),
@@ -271,10 +303,10 @@
             pltpu.VMEM((queries, total), bf16),
             dma((3,)), dma((CHUNKS,)),
             dma((5, HALVES)), dma((4, HALVES)), dma((4, HALVES)), dma((4, HALVES)),
-            dma((2, CHUNKS)), dma((2, CHUNKS)), dma((CHUNKS,)), dma((CHUNKS,)),
+            dma((2, tiles)), dma((2, tiles)), dma((tiles,)), dma((tiles,)),
         ],
         compiler_params=pltpu.CompilerParams(
-            collective_id=0, has_side_effects=True, vmem_limit_bytes=60 * 2**20
+            collective_id=0, has_side_effects=True, vmem_limit_bytes=50 * 2**20
         ),
     )(row_grads, query_grads, fisher_inv)
     return out.T

time: 31.2 us -> 29.4 us (0.942)
  Pallas kernels: 29.1 us -> 27.5 us
    pallas_call x1, Pallas kernels: 29.1 us -> 27.5 us  [fused(): pl.pallas_call(kernel, out_shape=jax.ShapeDtypeStruct((queries, total), j...]
    unnamed x1 -> x3, local copies, waits for them, and re-layouts: 1.87 us -> 1.75 us
where the time goes in v3:
time: 29.4 us; the launch traced here: 29.2 us
  Pallas kernels  27.5 us (94%)
  local copies, waits for them, and re-layouts  1.75 us (6%)
    pallas_call x1, Pallas kernels, fused(): pl.pallas_call(kernel, out_shape=jax.ShapeDtypeStruct((queries, total), j...  27.5 us
    unnamed x3, local copies, waits for them, and re-layouts  1.75 us

profile of v3, /device:TPU:24, one launch (start us, length us, event | category | flops | bytes accessed | tf_op | source)
XLA Modules:
  0.0 29.2 jit_solution(4299529617646535035)
XLA Ops:
  0.0 0.0 copy-start
  0.0 0.9 %copy-done = bf16[2,64,1024]{2,1,0:T(8,128)(2,1)S(1)} copy-done((bf16[2,64,1024]{2,1,0:T(8,128)(2,1)S(1)}, bf16[2,64,1024]{2,1,0:T(8,128)(2,1)}, u32[]{:S(2)}) %copy-start) | copy-done | bytes 262168
  1.0 27.5 %shard_map.37 = f32[64,2048]{1,0:T(8,128)S(1)} custom-call(bf16[2,2048,1024]{2,1,0:T(8,128)(2,1)} %rows_hbm.1, bf16[2,64,1024]{2,1,0:T(8,128)(2,1)S(1)} %copy-done, bf16[2,1024,1024]{2,1,0:T(8,128)(2,1)} %f_hbm.1), custom_call_target="tpu_custom_call" | custom-call | tf_op jit(solution)/shard_map/pallas_call | solution.py:288
  28.4 0.8 %copy.5 = f32[2048,64]{0,1:T(8,128)} copy(f32[2048,64]{0,1:T(8,128)S(1)} %bitcast.1) | data formatting | bytes 1048576
Async XLA Ops:
  0.0 0.9 %copy-start = (bf16[2,64,1024]{2,1,0:T(8,128)(2,1)S(1)}, bf16[2,64,1024]{2,1,0:T(8,128)(2,1)}, u32[]{:S(2)}) copy-start(bf16[2,64,1024]{2,1,0:T(8,128)(2,1)} %q_hbm.1) | copy-start | bytes 786436

commit v4 on v3

--- a/solution.py
+++ b/solution.py
@@ -63,6 +63,9 @@
         part = pl.ds(n * step, step)
         return pltpu.make_async_copy(rows_hbm.at[:, part], rows.at[:, part], row_sem.at[n])
 
+    for n in range(CHUNKS):
+        row_copy(n).start()
+
     barrier = pltpu.get_barrier_semaphore()
 
     def greet(**device):
@@ -95,20 +98,21 @@
 
     onward = {1: order[2], 2: order[1], 3: order[1]}
 
+    def z_half(k, h):
+        z_copy(order[k], order[1], 1 + k, h).wait_recv()
+
+        @pl.when(mid)
+        def _():
+            z_copy(order[k], onward[k], 1 + k, h).start()
+
+        y_copy(k, y, h).start()
+
     def pass_on(k):
         for h in range(HALVES):
-            z_copy(order[k], order[1], 1 + k, h).wait_recv()
-
-            @pl.when(mid)
-            def _():
-                z_copy(order[k], onward[k], 1 + k, h).start()
-
-            y_copy(k, y, h).start()
+            z_half(k, h)
 
     loads[0].wait()
     loads[1].wait()
-    for n in range(CHUNKS):
-        row_copy(n).start()
     prep[z, y] = dot_nt(q[y], fisher[0]).astype(jnp.bfloat16)
     pl.semaphore_wait(barrier, 4 + w)
     for h in range(HALVES):
@@ -206,25 +210,33 @@
     def _():
         pass_on(2)
 
+    first(1)
+
+    @pl.when(mid)
+    def _():
+        pass_on(3)
+
+    @pl.when(jnp.logical_not(mid))
+    def _():
+        pass_on(2)
+
+    first(2)
     each(0, (reduce, 0))
-    first(1)
-
-    @pl.when(mid)
-    def _():
-        pass_on(3)
+    for h in range(HALVES):
+        swapped(1, h)
+    second(1, 0, 0)
 
     @pl.when(jnp.logical_not(mid))
     def _():
-        pass_on(2)
-
-    first(2)
-    for h in range(HALVES):
-        swapped(1, h)
-    each(1, (second, 0))
+        z_half(3, 0)
+
+    for n in range(1, CHUNKS):
+        second(1, 0, n)
 
     @pl.when(jnp.logical_not(mid))
     def _():
-        pass_on(3)
+        for n in range(1, HALVES):
+            z_half(3, n)
 
     first(3)
     each(1, (reduce, 0))

time: 29.4 us -> 29.5 us (level)
  no operation moved by 1% of the time
where the time goes in v4:
time: 29.5 us; the launch traced here: 29.3 us
  Pallas kernels  27.6 us (94%)
  local copies, waits for them, and re-layouts  1.75 us (6%)
    pallas_call x1, Pallas kernels, fused(): pl.pallas_call(kernel, out_shape=jax.ShapeDtypeStruct((queries, total), j...  27.6 us
    unnamed x3, local copies, waits for them, and re-layouts  1.75 us

profile of v4, /device:TPU:24, one launch (start us, length us, event | category | flops | bytes accessed | tf_op | source)
XLA Modules:
  0.0 29.3 jit_solution(215802333452017649)
XLA Ops:
  0.0 0.0 copy-start
  0.0 0.9 %copy-done = bf16[2,64,1024]{2,1,0:T(8,128)(2,1)S(1)} copy-done((bf16[2,64,1024]{2,1,0:T(8,128)(2,1)S(1)}, bf16[2,64,1024]{2,1,0:T(8,128)(2,1)}, u32[]{:S(2)}) %copy-start) | copy-done | bytes 262168
  1.0 27.6 %shard_map.37 = f32[64,2048]{1,0:T(8,128)S(1)} custom-call(bf16[2,2048,1024]{2,1,0:T(8,128)(2,1)} %rows_hbm.1, bf16[2,64,1024]{2,1,0:T(8,128)(2,1)S(1)} %copy-done, bf16[2,1024,1024]{2,1,0:T(8,128)(2,1)} %f_hbm.1), custom_call_target="tpu_custom_call" | custom-call | tf_op jit(solution)/shard_map/pallas_call | solution.py:300
  28.5 0.8 %copy.5 = f32[2048,64]{0,1:T(8,128)} copy(f32[2048,64]{0,1:T(8,128)S(1)} %bitcast.1) | data formatting | bytes 1048576
Async XLA Ops:
  0.0 0.9 %copy-start = (bf16[2,64,1024]{2,1,0:T(8,128)(2,1)S(1)}, bf16[2,64,1024]{2,1,0:T(8,128)(2,1)}, u32[]{:S(2)}) copy-start(bf16[2,64,1024]{2,1,0:T(8,128)(2,1)} %q_hbm.1) | copy-start | bytes 786436
